TPU v7x, 512 devices: a whole 4x4x16 slice. The times are simulated.
512 devices in a mesh: dp: 8 (over x, core), space: 64 (over z, y).
Axes of the slice: x: 4, y: 4, z: 16, core: 2. Of those that a mesh axis runs over, the one named last changes fastest.
Arguments:
- features: bfloat16 [8, 65536, 256], P('dp', 'space'), may hold values from -6 to 6
- weight: bfloat16 [2048, 256], P(('dp', 'space')), may hold values from -0.125 to 0.125
- rulebook: int32 [8, 512, 3, 8], P('dp', 'space'), may hold values from 0 to 63, as said below
- rule_counts: int32 [8, 512], P('dp', 'space'), may hold values from 1 to 8, as said below
- cotangent: bfloat16 [8, 32768, 256], P('dp', 'space'), may hold values from -6 to 6
Outputs:
- activated: bfloat16 [8, 32768, 256], P('dp', 'space')
- grad_features: bfloat16 [8, 65536, 256], P('dp', 'space')
- grad_weight: float32 [2048, 256], P(('dp', 'space'))
Inputs may be any that keep to these rules, and one draw needn't show every extreme that they name: `rulebook`: in the row of slab s the owner is s - 1, s or s + 1 and lies in 0 to 63; the input block lies in 0 to 7; the output block lies in 0 to 3, and in 2 to 3 when the owner is s - 1, in 0 to 1 when it is s + 1. Padded slots hold entries of the same kind. A block may appear in several rules. `rule_counts`: some slab and offset has 8 live rules in every draw.
All inputs are finite; a program needn't handle non-finite values.
Results may differ from a plain program's by a relative error of at most 0.0049.
Values may be sent and summed in bfloat16 or wider, within the bound.
A program may use at most 64 MiB of HBM per device.

v0:
```python
import jax
import jax.numpy as jnp
from jax import lax
from jax.sharding import PartitionSpec as P

CI = 256
CO = 256
OFFS = 8
BR = 128
BND = 2
SLOTS = 8
IN_BLK = 8
OUT_BLK = 4


grad_scale = 1.0 / 2048.0


def from_behind(value, axis, steps):
    count = lax.axis_size(axis)
    first, last = (max(0, -steps), min(count, count - steps))
    return lax.ppermute(value, axis, [(source, source + steps) for source in range(first, last)])


def with_halo(block, sides, width):
    for axis, dim in sides:
        count = lax.axis_size(axis)
        forward = [(i, i + 1) for i in range(count - 1)]
        backward = [(target, source) for source, target in forward]
        low = lax.ppermute(
            lax.slice_in_dim(block, block.shape[dim] - width, None, axis=dim), axis, forward
        )
        high = lax.ppermute(lax.slice_in_dim(block, 0, width, axis=dim), axis, backward)
        block = jnp.concatenate([low, block, high], axis=dim)
    return block


def local(features, weight, rulebook, rule_counts, cotangent):
    position = lax.axis_index("space")
    blocks = features[0].reshape(IN_BLK, BR, CI)
    full_weight = lax.all_gather(weight, ("dp", "space"), axis=0, tiled=True).reshape(OFFS, CI, CO)
    extent = OUT_BLK + 2 * BND
    slot_ids = jnp.arange(SLOTS, dtype=jnp.int32)
    partial_out = jnp.zeros((extent + 1, BR, CO), jnp.float32)
    saved = []
    for offset in range(OFFS):
        in_index = rulebook[0, offset, 0]
        out_index = rulebook[0, offset, 1]
        relative = rulebook[0, offset, 2] - position
        slot = jnp.where(
            relative == 0,
            BND + out_index,
            jnp.where(relative < 0, out_index - (OUT_BLK - BND), BND + OUT_BLK + out_index),
        )
        live = slot_ids < rule_counts[0, offset]
        target = jnp.where(live, slot, extent)
        picked = blocks[in_index].reshape(SLOTS * BR, CI)
        product = jnp.dot(picked, full_weight[offset], preferred_element_type=jnp.float32).reshape(
            SLOTS, BR, CO
        )
        partial_out = partial_out + jax.ops.segment_sum(product, target, num_segments=extent + 1)
        saved.append((in_index, slot, live, picked))
    lower_send = partial_out[:BND]
    upper_send = partial_out[BND + OUT_BLK : extent]
    own_part = partial_out[BND : BND + OUT_BLK]
    from_below = from_behind(upper_send, "space", 1)
    from_above = from_behind(lower_send, "space", -1)
    middle = jnp.zeros((OUT_BLK - 2 * BND, BR, CO), jnp.float32)
    summed = own_part + jnp.concatenate([from_below, middle, from_above], 0)
    sigma = jax.nn.sigmoid(summed)
    activated = (summed * sigma).astype(jnp.bfloat16)
    upstream = cotangent[0].reshape(OUT_BLK, BR, CO).astype(jnp.float32)
    grad_pre = (upstream * sigma * (1.0 + summed * (1.0 - sigma))).astype(jnp.bfloat16)
    grad_wide = with_halo(grad_pre, (("space", 0),), BND)
    grad_in = jnp.zeros((IN_BLK + 1, BR, CI), jnp.float32)
    grad_terms = []
    for offset in range(OFFS):
        in_index, slot, live, picked = saved[offset]
        rule_grads = (grad_wide[slot] * live.astype(jnp.bfloat16)[:, None, None]).reshape(
            SLOTS * BR, CO
        )
        back = lax.dot_general(
            rule_grads,
            full_weight[offset],
            (((1,), (1,)), ((), ())),
            preferred_element_type=jnp.float32,
        )
        source = jnp.where(live, in_index, IN_BLK)
        grad_in = grad_in + jax.ops.segment_sum(
            back.reshape(SLOTS, BR, CI), source, num_segments=IN_BLK + 1
        )
        grad_terms.append(
            lax.dot_general(
                picked, rule_grads, (((0,), (0,)), ((), ())), preferred_element_type=jnp.float32
            )
        )
    weight_term = jnp.concatenate(grad_terms, 0)
    reduced = lax.psum_scatter(weight_term, ("dp", "space"), scatter_dimension=0, tiled=True)
    grad_weight = reduced * grad_scale
    return (
        activated.reshape(1, OUT_BLK * BR, CO),
        grad_in[:IN_BLK].astype(jnp.bfloat16).reshape(1, IN_BLK * BR, CI),
        grad_weight,
    )


def solution(mesh):
    in_specs = (
        P("dp", "space", None),
        P(("dp", "space"), None),
        P("dp", "space", None, None),
        P("dp", "space"),
        P("dp", "space", None),
    )
    out_specs = (P("dp", "space", None), P("dp", "space", None), P(("dp", "space"), None))
    return jax.shard_map(local, mesh=mesh, in_specs=in_specs, out_specs=out_specs, check_vma=False)
```

profile of v0, /device:TPU:1, one launch (start us, length us, event | category | flops | bytes accessed | tf_op | source)
XLA Modules:
  0.0 770.6 jit_solution(16303449982079730345)
XLA Ops:
  8.0 1.6 fusion.102
  11.9 3.4 fusion.64
  16.5 1.4 gather_fusion.2
  17.9 1.4 gather_fusion.3
  19.3 1.4 gather_fusion.4
  21.3 1.4 gather_fusion.6
  22.7 1.4 gather_fusion.7
  24.1 1.3 compare_convert_fusion.7
  30.1 3.2 fusion.60
  35.7 1.9 fusion.51
  37.6 1.8 fusion.55
  39.4 1.8 fusion.57
  41.2 144.8 %all-gather.3.cloned.1.call-done = bf16[512,4,256]{2,1,0:T(4,128)(2,1)} async-done(((bf16[1,4,256]{2,1,0:T(4,128)(2,1)}), bf16[512,4,256]{2,1,0:T(4,128)(2,1)}) %all-gather.3.cloned.1.call-update) | async-done | bytes 1048592 | tf_op jit(solution)/shard_map/all_gather | solution.py:41
  186.0 1.6 fusion.100
  191.3 1.3 fusion.104
  193.6 2.5 scatter_fusion.1
  197.2 3.2 scatter_fusion
  200.3 1.5 add.589
  201.9 1.3 fusion.105
  203.5 2.6 scatter_fusion.2
  207.2 3.2 scatter_fusion.3
  210.4 1.5 add.596
  211.9 1.3 fusion.107
  213.5 2.6 scatter_fusion.4
  217.3 3.2 scatter_fusion.5
  220.4 1.5 add.603
  223.0 1.3 fusion.110
  224.3 1.3 scatter_fusion.6
  225.7 2.6 scatter_fusion.7
  228.5 3.5 collective-permute-start
  232.0 1.3 collective-permute-start.1
  235.1 2.3 collective-permute-done
  237.4 3.8 collective-permute-done.1
  242.2 3.2 collective-permute-start.2
  245.5 1.5 collective-permute-start.3
  248.7 2.4 collective-permute-done.3
  253.8 1.4 fusion.33
  255.2 1.6 gather_fusion.9
  256.9 2.5 fusion.30
  260.5 1.7 gather_fusion.10
  262.1 2.4 fusion.27
  265.7 1.4 gather_fusion.11
  267.1 2.4 fusion.24
  270.6 1.4 gather_fusion.12
  272.0 2.5 fusion.21
  275.7 1.5 gather_fusion.13
  277.2 1.6 gather_fusion.14
  278.8 1.4 gather_fusion.15
  280.2 2.2 fusion.2
  285.4 2.5 scatter_fusion.9
  289.0 3.2 scatter_fusion.8
  292.2 1.4 add.616
  293.6 2.5 scatter_fusion.10
  297.7 3.2 scatter_fusion.11
  301.0 1.4 add.619
  302.4 2.5 scatter_fusion.12
  304.9 1.3 fusion.18
  306.4 2.5 scatter_fusion.13
  308.9 1.3 add.622
  311.4 1.3 scatter_fusion.14
  312.7 1.4 fusion.12
  314.2 2.5 scatter_fusion.15
  317.6 444.9 %all-reduce.3.cloned.1.call-done = f32[2048,256]{1,0:T(8,128)} async-done(((f32[2048,256]{1,0:T(8,128)}), f32[2048,256]{1,0:T(8,128)}) %all-reduce.3.cloned.1.call-update) | async-done | bytes 2097168
  762.4 1.3 dynamic-slice_multiply_fusion
  (199 shorter events, 41.7 us)
Async XLA Ops:
  7.2 8.2 %copy-start = (bf16[1,1024,256]{2,1,0:T(8,128)(2,1)S(1)}, bf16[1,1024,256]{2,1,0:T(8,128)(2,1)}, u32[]{:S(2)}) copy-start(bf16[1,1024,256]{2,1,0:T(8,128)(2,1)} %param.5) | copy-start | bytes 1572868
  7.2 178.8 %all-gather.3.cloned.1.call-start = ((), (), s32[]{:S(2)}) async-start(), calls=%async_computation | async-start | bytes 1050624 | tf_op jit(solution)/shard_map/all_gather | solution.py:41
  7.9 754.5 %all-reduce.3.cloned.1.call-start = ((), (), s32[]{:S(2)}) async-start(), calls=%async_computation.1 | async-start | bytes 4194304
  15.9 175.4 %copy-start.11 = (bf16[8,128,256]{2,1,0:T(8,128)(2,1)}, bf16[8,128,256]{2,1,0:T(8,128)(2,1)S(1)}, u32[]{:S(2)}) copy-start(bf16[8,128,256]{2,1,0:T(8,128)(2,1)S(1)} %gather_fusion.1) | copy-start | bytes 1572868
  16.5 176.1 %copy-start.15 = (bf16[8,128,256]{2,1,0:T(8,128)(2,1)}, bf16[8,128,256]{2,1,0:T(8,128)(2,1)S(1)}, u32[]{:S(2)}) copy-start(bf16[8,128,256]{2,1,0:T(8,128)(2,1)S(1)} %gather_fusion) | copy-start | bytes 1572868
  21.3 7.5 copy-start.41
  187.7 4.9 copy-start.36
  187.7 4.9 copy-start.38
  200.3 1.5 copy-start.13
  200.3 1.5 copy-start.34
  201.8 1.3 copy-start.9
  201.9 1.3 copy-start.32
  210.4 1.5 copy-start.7
  210.4 1.5 copy-start.30
  211.9 1.3 copy-start.28
  220.4 1.5 copy-start.3
  220.4 1.5 copy-start.26
  223.0 1.3 copy-start.67
  228.3 6.8 copy-start.42
  228.3 6.8 copy-start.43
  228.5 12.7 %copy-start.40 = (bf16[1,512,256]{2,1,0:T(8,128)(2,1)S(1)}, bf16[1,512,256]{2,1,0:T(8,128)(2,1)}, u32[]{:S(2)}) copy-start(bf16[1,512,256]{2,1,0:T(8,128)(2,1)} %param.9) | copy-start | bytes 786436
  228.5 8.9 %collective-permute-start = (f32[2,128,256]{2,1,0:T(8,128)S(1)}, f32[2,128,256]{2,1,0:T(8,128)S(1)}, u32[]{:S(2)}, u32[]{:S(2)}) collective-permute-start(f32[2,128,256]{2,1,0:T(8,128)S(1)} %get-tuple-element.21), channel_id=1, source_target_pairs={{0,1},{1,2},{2,3},{3,4},{4,5},{5,6},{6,7},{7,8},{8,9},{9,10},{10,1... | collective-permute-start | bytes 786440 | tf_op jit(solution)/shard_map/ppermute | solution.py:22
  232.0 9.2 %collective-permute-start.1 = (f32[2,128,256]{2,1,0:T(8,128)S(1)}, f32[2,128,256]{2,1,0:T(8,128)S(1)}, u32[]{:S(2)}, u32[]{:S(2)}) collective-permute-start(f32[2,128,256]{2,1,0:T(8,128)S(1)} %get-tuple-element.22), channel_id=1, source_target_pairs={{1,0},{2,1},{3,2},{4,3},{5,4},{6,5},{7,6},{8,7},{9,8},{10,9},{11,1... | collective-permute-start | bytes 786440 | tf_op jit(solution)/shard_map/ppermute | solution.py:22
  241.2 6.9 copy-start.44
  241.2 6.9 copy-start.45
  242.2 10.5 %copy-start.16 = (bf16[8,128,256]{2,1,0:T(8,128)(2,1)S(1)}, bf16[8,128,256]{2,1,0:T(8,128)(2,1)}, u32[]{:S(2)}) copy-start(bf16[8,128,256]{2,1,0:T(8,128)(2,1)} %copy-done.15) | copy-start | bytes 1572868
  242.2 10.4 %copy-start.63 = (bf16[8]{0:T(256)(128)(2,1)S(1)}, bf16[8]{0:T(256)(128)(2,1)}, u32[]{:S(2)}) copy-start(bf16[8]{0:T(256)(128)(2,1)} %compare_convert_fusion.7) | copy-start | bytes 52
  242.2 6.5 collective-permute-start.2
  245.5 5.7 collective-permute-start.3
  251.2 2.5 copy-start.39
  251.3 2.5 copy-start.64
  253.8 3.1 copy-start.37
  253.8 3.1 copy-start.62
  255.2 4.1 copy-start.12
  256.9 2.5 copy-start.21
  259.3 2.8 copy-start.35
  259.3 2.8 copy-start.61
  260.5 4.1 copy-start.14
  262.1 2.5 copy-start.22
  264.6 2.5 copy-start.33
  264.6 2.5 copy-start.59
  265.7 3.8 copy-start.10
  267.1 2.4 copy-start.23
  269.5 2.5 copy-start.31
  269.5 2.5 copy-start.60
  270.6 3.9 copy-start.8
  272.0 2.5 copy-start.24
  277.2 3.0 copy-start.58
  278.8 3.6 copy-start.4
  278.8 3.6 copy-start.65
  280.2 2.2 copy-start.18
  282.4 1.2 copy-start.17
  292.2 1.4 copy-start.50
  296.1 1.7 copy-start.2
  296.1 1.6 copy-start.48
  301.0 1.4 copy-start.49
  302.4 2.5 copy-start.20
  302.4 2.5 copy-start.29
  304.9 1.5 copy-start.47
  308.9 1.3 copy-start.19
  308.9 1.3 copy-start.27
  310.1 1.3 copy-start.1
  310.1 1.3 copy-start.46
  312.7 1.5 copy-start.57
  (10 other events, 10.1 us)
Sparse Core Ops, SparseCore 0:
  12.6 173.3 all-gather.2
  284.9 477.5 all-reduce.2
where the time goes:
time: 772 us; the launch traced here: 771 us
  waiting for transfers between devices  599 us (78%)
  other arithmetic  79.4 us (10%)
  local copies, waits for them, and re-layouts  37.3 us (5%)
  matrix products  30.7 us (4%)
  between operations  14.8 us (2%)
  starting transfers between devices  9.52 us (1%)
    unnamed x3, waiting for transfers between devices  446 us
    all_gather x1, waiting for transfers between devices, local(): lax.all_gather(weight, ('dp', 'space'), axis=0, tiled=True)  145 us
    scatter-add x8, other arithmetic, local(): jax.ops.segment_sum(product, target, num_segments=extent + 1)  21 us
    scatter-add x8, other arithmetic, local(): jax.ops.segment_sum(back.reshape(SLOTS, BR, CI), source, num_segments=IN_...  20 us
  transfers between devices with their start and end apart: 6, of which 5 were waited for; matrix products, arithmetic and copies ran while one was open for 9% of the time, Pallas kernels for 0%

commit v1 on v0

v1 whole, which is shorter than its diff:
```python
import functools

import jax
import jax.numpy as jnp
from jax import lax
from jax.experimental import pallas as pl
from jax.experimental.pallas import tpu as pltpu
from jax.sharding import PartitionSpec as P

OFFS = 8
BND = 2
SLOTS = 8
IN_BLK = 8
OUT_BLK = 4
EXT = OUT_BLK + 2 * BND
NONE = OFFS * SLOTS

grad_scale = 1.0 / 2048.0
BF16 = jnp.bfloat16
F32 = jnp.float32
MESH = pl.DeviceIdType.MESH

NX, NY, NZ = 4, 4, 16


def dot(a, b, dims):
    return lax.dot_general(a, b, (dims, ((), ())), preferred_element_type=F32)


NN = ((1,), (0,))
NT = ((1,), (1,))


def kernel(
    feat_hbm, w_ref, rules, counts, cot_hbm,
    act_hbm, gf_hbm, gw_ref,
    xin, xp, xt, cot, wz, wst, wf, yb, sums, hs, hr, gext, act, gfp,
    sb_send, sb_recv, own, xs, xr, ys, yr, zs, zr,
    f_in, f_prev, b_slot, b_prev, lasts,
    loc_sem, z_sem, y_sem, x_sem, c_sem, h_sem, rc_sem, rx_sem, ry_sem, rz_sem,
):
    ci = xin.shape[1]
    br = xp.shape[1]
    dp = lax.axis_index("dp")
    space = lax.axis_index("space")
    x, c = lax.div(dp, 2), lax.rem(dp, 2)
    z, y = lax.div(space, NY), lax.rem(space, NY)
    oc = 1 - c
    n_space = NY * NZ
    sib = (x * 2 + oc, space)
    up = (dp, lax.rem(space + 1, n_space))
    down = (dp, lax.rem(space + n_space - 1, n_space))

    def x_of(off):
        return lax.rem(x + off, NX)

    def at_x(off):
        return (x_of(off) * 2 + c, space)

    def at_y(off):
        return (dp, z * NY + lax.rem(y + off, NY))

    def at_z(off):
        return (dp, lax.rem(z + off, NZ) * NY + y)

    def remote(src, dst, sems, index, device):
        return pltpu.make_async_remote_copy(
            src_ref=src, dst_ref=dst, send_sem=sems.at[0, index], recv_sem=sems.at[1, index],
            device_id=device, device_id_type=MESH,
        )

    get_x = pltpu.make_async_copy(feat_hbm.at[0], xin, loc_sem.at[0])
    get_cot = pltpu.make_async_copy(cot_hbm.at[0], cot, loc_sem.at[1])
    get_x.start()
    get_cot.start()
    barrier = pltpu.get_barrier_semaphore()

    def greet(device):
        pl.semaphore_signal(barrier, inc=1, device_id=device, device_id_type=MESH)

    wz[0, 0:4, :] = w_ref[:, 0:128].astype(F32)
    wz[0, 4:8, :] = w_ref[:, 128:256].astype(F32)

    @pl.loop(1, NZ)
    def _(d):
        greet(at_z(d))

    for d in range(1, NY):
        greet(at_y(d))
    for d in range(1, NX):
        greet(at_x(d))
    for device in (sib, up, down):
        greet(device)
    pl.semaphore_wait(barrier, NZ + NY + NX)

    @pl.loop(1, NZ)
    def _(d):
        remote(wz.at[0], wz.at[d], z_sem, d, at_z(d)).start()

    get_x.wait()
    rows = lax.broadcasted_iota(jnp.int32, (ci, ci), 0)
    cols = lax.broadcasted_iota(jnp.int32, (ci, ci), 1)

    def channel(p):
        from_y = lax.rem(y + NY - lax.div(p, 4 * NZ), NY)
        from_z = lax.rem(z + NZ - lax.div(lax.rem(p, 4 * NZ), 4), NZ)
        return from_z * (4 * NY) + from_y * 4 + lax.rem(p, 4)

    perm = jnp.where(rows == channel(cols), 1.0, 0.0).astype(BF16)
    perm_t = jnp.where(cols == channel(rows), 1.0, 0.0).astype(BF16)

    @pl.loop(0, IN_BLK)
    def _(i):
        block = xin[pl.ds(pl.multiple_of(i * br, br), br), :]
        xp[i] = dot(block, perm, NN).astype(BF16)
        xt[i] = dot(perm_t, block, NT).astype(BF16)

    sums[NONE] = jnp.zeros(sums.shape[1:], F32)
    gext[EXT] = jnp.zeros(gext.shape[1:], BF16)

    def kernel_at(t):
        pair = t // 2
        off = pair + (pair // 2) * (1 - 2 * (pair % 2))
        return lax.rem(x + off, NX) * 2 + lax.rem(c + t % 2, 2)

    def chain(t, carry):
        f_last, b_last = list(carry[:EXT]), list(carry[EXT:])
        k = kernel_at(t)
        count = counts[0, k]
        for j in range(SLOTS):
            n = t * SLOTS + j
            source, block, owner = rules[0, k, 0, j], rules[0, k, 1, j], rules[0, k, 2, j]
            slot = BND + block + (owner - space) * OUT_BLK
            live = j < count
            slot = jnp.where(live, slot, EXT)
            start = jnp.where(live, source, IN_BLK)
            f_in[n] = source
            b_slot[n] = slot
            prev = jnp.int32(NONE)
            for o in range(EXT):
                hit = slot == o
                prev = jnp.where(hit, f_last[o], prev)
                f_last[o] = jnp.where(hit, n, f_last[o])
            f_prev[n] = prev
            prev = jnp.int32(NONE)
            for o in range(IN_BLK):
                hit = start == o
                prev = jnp.where(hit, b_last[o], prev)
                b_last[o] = jnp.where(hit, n, b_last[o])
            b_prev[n] = prev
        return tuple(f_last + b_last)

    ends = lax.fori_loop(0, OFFS, chain, (jnp.int32(NONE),) * (EXT + IN_BLK))
    for o in range(EXT + IN_BLK):
        lasts[o] = ends[o]

    @pl.loop(1, NZ)
    def _(d):
        remote(wz.at[0], wz.at[d], z_sem, d, at_z(d)).wait_recv()

    low = lax.broadcasted_iota(jnp.int32, (8, 128), 0) < 4
    for p in range(NZ // 2):
        a, b = wz[2 * p], wz[2 * p + 1]
        wst[8 * p : 8 * p + 8, 0:128] = jnp.where(low, a, pltpu.roll(b, 4, 0))
        wst[8 * p : 8 * p + 8, 128:256] = jnp.where(low, pltpu.roll(a, 4, 0), b)
    part = 4 * NZ
    wf[0, 0:part, :] = wst[...].astype(BF16)

    def y_copy(d):
        return remote(wf.at[0, pl.ds(0, part)], wf.at[0, pl.ds(d * part, part)], y_sem, d, at_y(d))

    for d in range(1, NY):
        y_copy(d).start()
    for d in range(1, NY):
        y_copy(d).wait_recv()

    order = (0, 1, 3, 2)

    def x_copy(d):
        return remote(wf.at[0], wf.at[2 * order.index(NX - d)], x_sem, d, at_x(d))

    def c_copy(off):
        t = 2 * order.index(off)
        return remote(wf.at[t], wf.at[t + 1], c_sem, off, sib)

    for d in (1, 3, 2):
        x_copy(d).start()
    c_copy(0).start()

    def arrive(off, other):
        if other:
            c_copy(off).wait_recv()
        elif off:
            x_copy(NX - off).wait_recv()
            c_copy(off).start()

    for t in range(OFFS):
        arrive(order[t // 2], t % 2 == 1)
        flat = xp[...].reshape(IN_BLK * br, ci)
        yb[...] = dot(flat, wf[t], NN).reshape(yb.shape)
        for j in range(SLOTS):
            n = t * SLOTS + j
            sums[n] = yb[f_in[n]] + sums[f_prev[n]]

    for i in range(BND):
        hs[i] = sums[lasts[i]].astype(BF16)
        hs[BND + i] = sums[lasts[BND + OUT_BLK + i]].astype(BF16)
    low_rim, high_rim = pl.ds(0, BND), pl.ds(BND, BND)
    remote(hs.at[low_rim], hr.at[high_rim], h_sem, 0, down).start()
    remote(hs.at[high_rim], hr.at[low_rim], h_sem, 1, up).start()
    get_cot.wait()
    remote(hs.at[high_rim], hr.at[low_rim], h_sem, 1, up).wait_recv()
    remote(hs.at[low_rim], hr.at[high_rim], h_sem, 0, down).wait_recv()
    for o in range(OUT_BLK):
        pre = sums[lasts[BND + o]] + hr[o].astype(F32)
        sigma = jax.nn.sigmoid(pre)
        act[o * br : (o + 1) * br, :] = (pre * sigma).astype(BF16)
        upstream = cot[o * br : (o + 1) * br, :].astype(F32)
        gext[BND + o] = (upstream * sigma * (1.0 + pre * (1.0 - sigma))).astype(BF16)
    own_low, own_high = pl.ds(BND, BND), pl.ds(OUT_BLK, BND)
    top, bottom = pl.ds(BND + OUT_BLK, BND), pl.ds(0, BND)
    remote(gext.at[own_low], gext.at[top], h_sem, 2, down).start()
    remote(gext.at[own_high], gext.at[bottom], h_sem, 3, up).start()
    put_act = pltpu.make_async_copy(act, act_hbm.at[0], loc_sem.at[2])
    put_act.start()
    remote(gext.at[own_low], gext.at[top], h_sem, 2, down).wait_recv()
    remote(gext.at[own_high], gext.at[bottom], h_sem, 3, up).wait_recv()

    def term(off, other):
        t = 2 * order.index(off) + int(other)
        lhs = [xt[f_in[t * SLOTS + j]] for j in range(SLOTS)]
        rhs = [gext[b_slot[t * SLOTS + j]] for j in range(SLOTS)]
        return dot(jnp.concatenate(lhs, axis=1), jnp.concatenate(rhs, axis=0), NN)

    def to_sibling(off):
        sb_send[off] = term(off, True)
        remote(sb_send.at[off], sb_recv.at[off], rc_sem, off, sib).start()

    sequence = (2, 1, 3, 0)
    to_sibling(sequence[0])
    for i, off in enumerate(sequence):
        own[...] = term(off, False)
        if i + 1 < NX:
            to_sibling(sequence[i + 1])
        remote(sb_send.at[off], sb_recv.at[off], rc_sem, off, sib).wait_recv()
        if off:
            xs[off] = (own[...] + sb_recv[off]).astype(BF16)
            remote(xs.at[off], xr.at[off], rx_sem, off, at_x(off)).start()
        else:
            own[...] += sb_recv[off]

    for t in range(OFFS):
        flat = gext[0:EXT].reshape(EXT * br, gext.shape[2])
        yb[:, :, 0:ci] = dot(flat, wf[t], NT).reshape(EXT, br, ci)
        for j in range(SLOTS):
            n = t * SLOTS + j
            place = jnp.minimum(b_slot[n], EXT - 1)
            sums[n] = yb[place] + sums[b_prev[n]]

    for d in range(1, NX):
        remote(xs.at[d], xr.at[d], rx_sem, d, at_x(d)).wait_recv()
    total = own[...]
    for d in range(1, NX):
        total = total + xr[d].astype(F32)
    own[...] = total
    for d in range(1, NY):
        ys[d] = own[(NY - d) * part : (NY - d + 1) * part, :].astype(BF16)
        remote(ys.at[d], yr.at[d], ry_sem, d, at_y(d)).start()

    for i in range(IN_BLK):
        back = sums[lasts[EXT + i]][:, 0:ci].astype(BF16)
        gfp[i * br : (i + 1) * br, :] = dot(back, perm_t, NN).astype(BF16)
    put_gf = pltpu.make_async_copy(gfp, gf_hbm.at[0], loc_sem.at[3])
    put_gf.start()

    for d in range(1, NY):
        remote(ys.at[d], yr.at[d], ry_sem, d, at_y(d)).wait_recv()
    total = own[0:part, :]
    for d in range(1, NY):
        total = total + yr[d].astype(F32)
    for p in range(NZ // 2):
        a, b = total[8 * p : 8 * p + 8, 0:128], total[8 * p : 8 * p + 8, 128:256]
        zs[2 * p] = jnp.where(low, a, pltpu.roll(b, 4, 0))
        zs[2 * p + 1] = jnp.where(low, pltpu.roll(a, 4, 0), b)

    @pl.loop(1, NZ)
    def _(d):
        remote(zs.at[NZ - d], zr.at[d], rz_sem, d, at_z(d)).start()

    @pl.loop(1, NZ)
    def _(d):
        remote(zs.at[NZ - d], zr.at[d], rz_sem, d, at_z(d)).wait_recv()

    total = zs[0]
    for d in range(1, NZ):
        total = total + zr[d]
    total = total * grad_scale
    gw_ref[:, 0:128] = total[0:4]
    gw_ref[:, 128:256] = total[4:8]

    @pl.loop(1, NZ)
    def _(d):
        remote(wz.at[0], wz.at[d], z_sem, d, at_z(d)).wait_send()
        remote(zs.at[NZ - d], zr.at[d], rz_sem, d, at_z(d)).wait_send()

    for d in range(1, NY):
        y_copy(d).wait_send()
        remote(ys.at[d], yr.at[d], ry_sem, d, at_y(d)).wait_send()
    for d in range(1, NX):
        x_copy(d).wait_send()
        remote(xs.at[d], xr.at[d], rx_sem, d, at_x(d)).wait_send()
    for off in range(NX):
        c_copy(off).wait_send()
        remote(sb_send.at[off], sb_recv.at[off], rc_sem, off, sib).wait_send()
    remote(hs.at[low_rim], hr.at[high_rim], h_sem, 0, down).wait_send()
    remote(hs.at[high_rim], hr.at[low_rim], h_sem, 1, up).wait_send()
    remote(gext.at[own_low], gext.at[top], h_sem, 2, down).wait_send()
    remote(gext.at[own_high], gext.at[bottom], h_sem, 3, up).wait_send()
    put_act.wait()
    put_gf.wait()


def local(features, weight, rulebook, rule_counts, cotangent):
    ci, co = features.shape[2], weight.shape[1]
    br = features.shape[1] // IN_BLK
    vmem = pl.BlockSpec(memory_space=pltpu.VMEM)
    smem = pl.BlockSpec(memory_space=pltpu.SMEM)
    hbm = pl.BlockSpec(memory_space=pl.ANY)
    dma = pltpu.SemaphoreType.DMA
    V = pltpu.VMEM
    return pl.pallas_call(
        kernel,
        out_shape=(
            jax.ShapeDtypeStruct(cotangent.shape, BF16),
            jax.ShapeDtypeStruct(features.shape, BF16),
            jax.ShapeDtypeStruct(weight.shape, F32),
        ),
        in_specs=[hbm, vmem, smem, smem, hbm],
        out_specs=(hbm, hbm, vmem),
        scratch_shapes=[
            V((IN_BLK * br, ci), BF16),
            V((IN_BLK, br, ci), BF16),
            V((IN_BLK, ci, br), BF16),
            V((OUT_BLK * br, co), BF16),
            V((NZ, 8, 128), F32),
            V((4 * NZ, co), F32),
            V((OFFS, ci, co), BF16),
            V((IN_BLK, br, max(ci, co)), F32),
            V((NONE + 1, br, max(ci, co)), F32),
            V((2 * BND, br, co), BF16),
            V((2 * BND, br, co), BF16),
            V((EXT + 1, br, co), BF16),
            V((OUT_BLK * br, co), BF16),
            V((IN_BLK * br, ci), BF16),
            V((NX, ci, co), F32),
            V((NX, ci, co), F32),
            V((ci, co), F32),
            V((NX, ci, co), BF16),
            V((NX, ci, co), BF16),
            V((NY, 4 * NZ, co), BF16),
            V((NY, 4 * NZ, co), BF16),
            V((NZ, 8, 128), F32),
            V((NZ, 8, 128), F32),
            pltpu.SMEM((NONE,), jnp.int32),
            pltpu.SMEM((NONE,), jnp.int32),
            pltpu.SMEM((NONE,), jnp.int32),
            pltpu.SMEM((NONE,), jnp.int32),
            pltpu.SMEM((EXT + IN_BLK,), jnp.int32),
            dma((4,)),
            dma((2, NZ)),
            dma((2, NY)),
            dma((2, NX)),
            dma((2, NX)),
            dma((2, 4)),
            dma((2, NX)),
            dma((2, NX)),
            dma((2, NY)),
            dma((2, NZ)),
        ],
        compiler_params=pltpu.CompilerParams(
            collective_id=0, has_side_effects=True, vmem_limit_bytes=48 * 1024 * 1024
        ),
    )(features, weight, rulebook, rule_counts, cotangent)


def solution(mesh):
    in_specs = (
        P("dp", "space", None),
        P(("dp", "space"), None),
        P("dp", "space", None, None),
        P("dp", "space"),
        P("dp", "space", None),
    )
    out_specs = (P("dp", "space", None), P("dp", "space", None), P(("dp", "space"), None))
    return jax.shard_map(local, mesh=mesh, in_specs=in_specs, out_specs=out_specs, check_vma=False)
```

time: 772 us -> 80.6 us (0.10)
  the two profiles are of different devices: /device:TPU:1 before, /device:TPU:8 now
where the time goes in v1:
time: 80.6 us; the launch traced here: 80.3 us
  Pallas kernels  74.9 us (93%)
  local copies, waits for them, and re-layouts  4.81 us (6%)
    pallas_call x1, Pallas kernels, local(): pl.pallas_call(kernel, out_shape=(jax.ShapeDtypeStruct(cotangent.shape, B...  74.9 us
    unnamed x12, local copies, waits for them, and re-layouts  4.81 us

profile of v1, /device:TPU:8, one launch (start us, length us, event | category | flops | bytes accessed | tf_op | source)
XLA Modules:
  0.0 80.3 jit_solution(10667125133693611161)
XLA Ops:
  0.6 0.0 copy-start.3
  0.6 0.0 copy-start.2
  0.7 0.7 copy.8.rules
  1.4 0.0 copy-done.3
  1.4 0.0 copy-done.2
  1.4 0.0 copy-start
  1.4 1.0 %copy-done = bf16[1,1024,256]{2,1,0:T(8,128)(2,1)S(1)} copy-done((bf16[1,1024,256]{2,1,0:T(8,128)(2,1)S(1)}, bf16[1,1024,256]{2,1,0:T(8,128)(2,1)}, u32[]{:S(2)}) %copy-start) | copy-done | bytes 524312
  2.4 0.0 copy-start.1
  2.4 0.9 %copy-done.1 = bf16[1,512,256]{2,1,0:T(8,128)(2,1)S(1)} copy-done((bf16[1,512,256]{2,1,0:T(8,128)(2,1)S(1)}, bf16[1,512,256]{2,1,0:T(8,128)(2,1)}, u32[]{:S(2)}) %copy-start.1) | copy-done | bytes 262168
  3.4 74.9 %shard_map.76 = (bf16[1,512,256]{2,1,0:T(8,128)(2,1)S(1)}, bf16[1,1024,256]{2,1,0:T(8,128)(2,1)S(1)}, f32[4,256]{1,0:T(4,128)S(1)}) custom-call(bf16[1,1024,256]{2,1,0:T(8,128)(2,1)S(1)} %copy-done, bf16[4,256]{1,0:T(4,128)(2,1)S(1)} %copy-done.2, s32[1,8,3,8]{3,2,1,0:T(4,128)S(1)} %copy.8.rules, s32[1,8]{1,0:T(1,128)S(1)} %copy-done.3, ...), custom_call_target="tpu_custom_call" | custom-call | tf_op jit(solution)/shard_map/pallas_call | solution.py:331
  78.3 0.7 copy.12
  79.0 0.8 copy.13
  79.8 0.6 copy.14
Async XLA Ops:
  0.6 0.7 copy-start.3
  0.6 0.7 copy-start.2
  1.4 1.0 %copy-start = (bf16[1,1024,256]{2,1,0:T(8,128)(2,1)S(1)}, bf16[1,1024,256]{2,1,0:T(8,128)(2,1)}, u32[]{:S(2)}) copy-start(bf16[1,1024,256]{2,1,0:T(8,128)(2,1)} %feat_hbm.1) | copy-start | bytes 1572868
  2.4 0.9 %copy-start.1 = (bf16[1,512,256]{2,1,0:T(8,128)(2,1)S(1)}, bf16[1,512,256]{2,1,0:T(8,128)(2,1)}, u32[]{:S(2)}) copy-start(bf16[1,512,256]{2,1,0:T(8,128)(2,1)} %cot_hbm.1) | copy-start | bytes 786436

commit v2 on v1

v2 whole, which is shorter than its diff:
```python
import functools

import jax
import jax.numpy as jnp
from jax import lax
from jax.experimental import pallas as pl
from jax.experimental.pallas import tpu as pltpu
from jax.sharding import PartitionSpec as P

OFFS = 8
BND = 2
SLOTS = 8
IN_BLK = 8
OUT_BLK = 4
EXT = OUT_BLK + 2 * BND
NONE = OFFS * SLOTS

grad_scale = 1.0 / 2048.0
BF16 = jnp.bfloat16
F32 = jnp.float32
MESH = pl.DeviceIdType.MESH

NX, NY, NZ = 4, 4, 16
REACH = 4


def dot(a, b, dims):
    return lax.dot_general(a, b, (dims, ((), ())), preferred_element_type=F32)


NN = ((1,), (0,))
NT = ((1,), (1,))


def kernel(
    feat_hbm, w_hbm, rules_hbm, counts_hbm, cot_hbm,
    act_hbm, gf_hbm, gw_hbm,
    xin, win, rules, counts, xp, xt, cot, wz, wst, wf, yb, sums, hs, hr, gext, act_ref, gf_ref, gw_ref,
    sb_send, sb_recv, own, xs, xr, ys, yr, zs, zr,
    f_in, f_prev, b_slot, b_prev, lasts,
    loc_sem, z_sem, y_sem, x_sem, c_sem, h_sem, rc_sem, rx_sem, ry_sem, rz_sem,
):
    ci = xin.shape[2]
    br = xp.shape[1]
    dp = lax.axis_index("dp")
    space = lax.axis_index("space")
    x, c = lax.div(dp, 2), lax.rem(dp, 2)
    z, y = lax.div(space, NY), lax.rem(space, NY)
    oc = 1 - c
    n_space = NY * NZ
    sib = (x * 2 + oc, space)
    up = (dp, lax.rem(space + 1, n_space))
    down = (dp, lax.rem(space + n_space - 1, n_space))

    def x_of(off):
        return lax.rem(x + off, NX)

    def at_x(off):
        return (x_of(off) * 2 + c, space)

    def at_y(off):
        return (dp, z * NY + lax.rem(y + off, NY))

    def at_z(off):
        return (dp, lax.rem(z + off, NZ) * NY + y)

    def remote(src, dst, sems, index, device):
        return pltpu.make_async_remote_copy(
            src_ref=src, dst_ref=dst, send_sem=sems.at[0, index], recv_sem=sems.at[1, index],
            device_id=device, device_id_type=MESH,
        )

    pending = []

    def send(copy):
        copy.start()
        pending.append(copy.wait_send)

    def put(src, dst, index):
        copy = pltpu.make_async_copy(src, dst, loc_sem.at[index])
        copy.start()
        pending.append(copy.wait)

    get_w = pltpu.make_async_copy(w_hbm, win, loc_sem.at[0])
    get_x = pltpu.make_async_copy(feat_hbm, xin, loc_sem.at[1])
    get_rules = pltpu.make_async_copy(rules_hbm, rules, loc_sem.at[2])
    get_counts = pltpu.make_async_copy(counts_hbm, counts, loc_sem.at[3])
    get_cot = pltpu.make_async_copy(cot_hbm.at[0], cot.at[pl.ds(BND, OUT_BLK)], loc_sem.at[4])
    for copy in (get_w, get_x, get_rules, get_counts, get_cot):
        copy.start()
    barrier = pltpu.get_barrier_semaphore()

    def greet(device):
        pl.semaphore_signal(barrier, inc=1, device_id=device, device_id_type=MESH)

    for d in (*range(1, REACH + 1), *range(NZ - REACH, NZ)):
        greet(at_z(d))
    for d in range(1, NY):
        greet(at_y(d))
    for d in range(1, NX):
        greet(at_x(d))
    for device in (sib, up, down):
        greet(device)
    get_w.wait()
    wz[0, 0:4, :] = win[:, 0:128].astype(F32)
    wz[0, 4:8, :] = win[:, 128:256].astype(F32)
    pl.semaphore_wait(barrier, 2 * REACH + 1 + NY + NX)

    def z_copy(d):
        return remote(wz.at[0], wz.at[d], z_sem, d, at_z(d))

    def each_z(act):
        pl.loop(1, NZ)(act)

    def z_pass(forward):
        if forward:
            src, dst, d = pl.ds(1, REACH), pl.ds(REACH + 1, REACH), REACH
        else:
            src, dst, d = pl.ds(NZ - REACH + 1, REACH - 1), pl.ds(NZ - 2 * REACH + 1, REACH - 1), NZ - REACH
        return remote(wz.at[src], wz.at[dst], z_sem, NZ + int(forward), at_z(d))

    for d in range(REACH, 0, -1):
        send(z_copy(d))
        send(z_copy(NZ - d))

    own_low, own_high = pl.ds(BND, BND), pl.ds(OUT_BLK, BND)
    top, bottom = pl.ds(BND + OUT_BLK, BND), pl.ds(0, BND)
    get_cot.wait()
    send(remote(cot.at[own_low], cot.at[top], h_sem, 0, down))
    send(remote(cot.at[own_high], cot.at[bottom], h_sem, 1, up))

    get_x.wait()
    rows = lax.broadcasted_iota(jnp.int32, (ci, ci), 0)
    cols = lax.broadcasted_iota(jnp.int32, (ci, ci), 1)

    def channel(p):
        from_y = lax.rem(y + NY - lax.div(p, 4 * NZ), NY)
        from_z = lax.rem(z + NZ - lax.div(lax.rem(p, 4 * NZ), 4), NZ)
        return from_z * (4 * NY) + from_y * 4 + lax.rem(p, 4)

    perm = jnp.where(rows == channel(cols), 1.0, 0.0).astype(BF16)
    perm_t = jnp.where(cols == channel(rows), 1.0, 0.0).astype(BF16)

    @pl.loop(0, IN_BLK)
    def _(i):
        block = xin[0, pl.ds(pl.multiple_of(i * br, br), br), :]
        xp[i] = dot(block, perm, NN).astype(BF16)
        xt[i] = dot(perm_t, block, NT).astype(BF16)

    sums[NONE] = jnp.zeros(sums.shape[1:], F32)
    gext[EXT] = jnp.zeros(gext.shape[1:], BF16)

    def kernel_at(t):
        pair = t // 2
        off = pair + (pair // 2) * (1 - 2 * (pair % 2))
        return lax.rem(x + off, NX) * 2 + lax.rem(c + t % 2, 2)

    def chain(t, carry):
        f_last, b_last = list(carry[:EXT]), list(carry[EXT:])
        k = kernel_at(t)
        count = counts[0, k]
        for j in range(SLOTS):
            n = t * SLOTS + j
            source, block, owner = rules[0, 0, k, j], rules[0, 1, k, j], rules[0, 2, k, j]
            slot = BND + block + (owner - space) * OUT_BLK
            live = j < count
            slot = jnp.where(live, slot, EXT)
            start = jnp.where(live, source, IN_BLK)
            f_in[n] = source
            b_slot[n] = slot
            prev = jnp.int32(NONE)
            for o in range(EXT):
                hit = slot == o
                prev = jnp.where(hit, f_last[o], prev)
                f_last[o] = jnp.where(hit, n, f_last[o])
            f_prev[n] = prev
            prev = jnp.int32(NONE)
            for o in range(IN_BLK):
                hit = start == o
                prev = jnp.where(hit, b_last[o], prev)
                b_last[o] = jnp.where(hit, n, b_last[o])
            b_prev[n] = prev
        return tuple(f_last + b_last)

    get_rules.wait()
    get_counts.wait()
    ends = lax.fori_loop(0, OFFS, chain, (jnp.int32(NONE),) * (EXT + IN_BLK))
    for o in range(EXT + IN_BLK):
        lasts[o] = ends[o]

    for d in range(1, REACH + 1):
        z_copy(d).wait_recv()
    send(z_pass(True))
    for d in range(NZ - 1, NZ - REACH - 1, -1):
        z_copy(d).wait_recv()
    if REACH > 1:
        send(z_pass(False))
        z_pass(False).wait_recv()
    z_pass(True).wait_recv()

    low = lax.broadcasted_iota(jnp.int32, (8, 128), 0) < 4
    for p in range(NZ // 2):
        a, b = wz[2 * p], wz[2 * p + 1]
        wst[8 * p : 8 * p + 8, 0:128] = jnp.where(low, a, pltpu.roll(b, 4, 0))
        wst[8 * p : 8 * p + 8, 128:256] = jnp.where(low, pltpu.roll(a, 4, 0), b)
    part = 4 * NZ
    wf[0, 0:part, :] = wst[...].astype(BF16)

    def y_copy(d):
        return remote(wf.at[0, pl.ds(0, part)], wf.at[0, pl.ds(d * part, part)], y_sem, d, at_y(d))

    for d in range(1, NY):
        send(y_copy(d))
    for d in range(1, NY):
        y_copy(d).wait_recv()

    order = (0, 1, 3, 2)

    def x_copy(d):
        return remote(wf.at[0], wf.at[2 * order.index(NX - d)], x_sem, d, at_x(d))

    def c_copy(off):
        t = 2 * order.index(off)
        return remote(wf.at[t], wf.at[t + 1], c_sem, off, sib)

    for d in (1, 3, 2):
        send(x_copy(d))
    send(c_copy(0))

    def arrive(off, other):
        if other:
            c_copy(off).wait_recv()
        elif off:
            x_copy(NX - off).wait_recv()
            send(c_copy(off))

    for t in range(OFFS):
        arrive(order[t // 2], t % 2 == 1)
        flat = xp[...].reshape(IN_BLK * br, ci)
        yb[...] = dot(flat, wf[t], NN).reshape(yb.shape)
        for j in range(SLOTS):
            n = t * SLOTS + j
            sums[n] = yb[f_in[n]] + sums[f_prev[n]]

    for i in range(EXT):
        hs[i] = sums[lasts[i]].astype(BF16)

    def rim_copy(half, upward):
        src = (OUT_BLK if upward else 0) + BND * half
        dst = src - OUT_BLK if upward else src + OUT_BLK
        index = 2 + 2 * int(upward) + half
        return remote(hs.at[pl.ds(src, BND)], hr.at[pl.ds(dst, BND)], h_sem, index, up if upward else down)

    for half in (0, 1):
        send(rim_copy(half, False))
        send(rim_copy(half, True))
    remote(cot.at[own_low], cot.at[top], h_sem, 0, down).wait_recv()
    remote(cot.at[own_high], cot.at[bottom], h_sem, 1, up).wait_recv()
    for half in (0, 1):
        for upward in (True, False):
            rim_copy(half, upward).wait_recv()
            first = (0 if upward else OUT_BLK) + BND * half
            for o in range(first, first + BND):
                pre = sums[lasts[o]] + hr[o].astype(F32)
                sigma = jax.nn.sigmoid(pre)
                if BND <= o < BND + OUT_BLK:
                    act_ref[0, (o - BND) * br : (o - BND + 1) * br, :] = (pre * sigma).astype(BF16)
                upstream = cot[o].astype(F32)
                gext[o] = (upstream * sigma * (1.0 + pre * (1.0 - sigma))).astype(BF16)
    put(act_ref, act_hbm, 5)

    def term(off, other):
        t = 2 * order.index(off) + int(other)
        lhs = [xt[f_in[t * SLOTS + j]] for j in range(SLOTS)]
        rhs = [gext[b_slot[t * SLOTS + j]] for j in range(SLOTS)]
        return dot(jnp.concatenate(lhs, axis=1), jnp.concatenate(rhs, axis=0), NN)

    def to_sibling(off):
        sb_send[off] = term(off, True)
        send(remote(sb_send.at[off], sb_recv.at[off], rc_sem, off, sib))

    sequence = (2, 1, 3, 0)
    to_sibling(sequence[0])
    for i, off in enumerate(sequence):
        own[...] = term(off, False)
        if i + 1 < NX:
            to_sibling(sequence[i + 1])
        remote(sb_send.at[off], sb_recv.at[off], rc_sem, off, sib).wait_recv()
        if off:
            xs[off] = (own[...] + sb_recv[off]).astype(BF16)
            send(remote(xs.at[off], xr.at[off], rx_sem, off, at_x(off)))
        else:
            own[...] += sb_recv[off]

    for t in range(OFFS):
        flat = gext[0:EXT].reshape(EXT * br, gext.shape[2])
        yb[:, :, 0:ci] = dot(flat, wf[t], NT).reshape(EXT, br, ci)
        for j in range(SLOTS):
            n = t * SLOTS + j
            place = jnp.minimum(b_slot[n], EXT - 1)
            sums[n] = yb[place] + sums[b_prev[n]]

    for d in range(1, NX):
        remote(xs.at[d], xr.at[d], rx_sem, d, at_x(d)).wait_recv()
    total = own[...]
    for d in range(1, NX):
        total = total + xr[d].astype(F32)
    own[...] = total
    for d in range(1, NY):
        ys[d] = own[(NY - d) * part : (NY - d + 1) * part, :].astype(BF16)
        send(remote(ys.at[d], yr.at[d], ry_sem, d, at_y(d)))

    for i in range(IN_BLK):
        back = sums[lasts[EXT + i]][:, 0:ci].astype(BF16)
        gf_ref[0, i * br : (i + 1) * br, :] = dot(back, perm_t, NN).astype(BF16)

    put(gf_ref, gf_hbm, 6)

    for d in range(1, NY):
        remote(ys.at[d], yr.at[d], ry_sem, d, at_y(d)).wait_recv()
    total = own[0:part, :]
    for d in range(1, NY):
        total = total + yr[d].astype(F32)
    for p in range(NZ // 2):
        a, b = total[8 * p : 8 * p + 8, 0:128], total[8 * p : 8 * p + 8, 128:256]
        zs[2 * p] = jnp.where(low, a, pltpu.roll(b, 4, 0))
        zs[2 * p + 1] = jnp.where(low, pltpu.roll(a, 4, 0), b)

    def out_copy(d):
        return remote(zs.at[NZ - d], zr.at[d], rz_sem, d, at_z(d))

    each_z(lambda d: out_copy(d).start())
    pending.append(lambda: each_z(lambda d: out_copy(d).wait_send()))
    each_z(lambda d: out_copy(d).wait_recv())

    total = zs[0]
    for d in range(1, NZ):
        total = total + zr[d]
    total = total * grad_scale
    gw_ref[:, 0:128] = total[0:4]
    gw_ref[:, 128:256] = total[4:8]

    put(gw_ref, gw_hbm, 7)
    for wait in pending:
        wait()


def local(features, weight, rulebook, rule_counts, cotangent):
    ci, co = features.shape[2], weight.shape[1]
    br = features.shape[1] // IN_BLK
    hbm = pl.BlockSpec(memory_space=pl.ANY)
    rules = jnp.transpose(rulebook, (0, 2, 1, 3))
    dma = pltpu.SemaphoreType.DMA
    V = pltpu.VMEM
    return pl.pallas_call(
        kernel,
        out_shape=(
            jax.ShapeDtypeStruct(cotangent.shape, BF16),
            jax.ShapeDtypeStruct(features.shape, BF16),
            jax.ShapeDtypeStruct(weight.shape, F32),
        ),
        in_specs=[hbm] * 5,
        out_specs=(hbm, hbm, hbm),
        scratch_shapes=[
            V(features.shape, BF16),
            V(weight.shape, BF16),
            pltpu.SMEM(rules.shape, jnp.int32),
            pltpu.SMEM(rule_counts.shape, jnp.int32),
            V((IN_BLK, br, ci), BF16),
            V((IN_BLK, ci, br), BF16),
            V((EXT, br, co), BF16),
            V((NZ, 8, 128), F32),
            V((4 * NZ, co), F32),
            V((OFFS, ci, co), BF16),
            V((IN_BLK, br, max(ci, co)), F32),
            V((NONE + 1, br, max(ci, co)), F32),
            V((EXT, br, co), BF16),
            V((EXT, br, co), BF16),
            V((EXT + 1, br, co), BF16),
            V(cotangent.shape, BF16),
            V(features.shape, BF16),
            V(weight.shape, F32),
            V((NX, ci, co), F32),
            V((NX, ci, co), F32),
            V((ci, co), F32),
            V((NX, ci, co), BF16),
            V((NX, ci, co), BF16),
            V((NY, 4 * NZ, co), BF16),
            V((NY, 4 * NZ, co), BF16),
            V((NZ, 8, 128), F32),
            V((NZ, 8, 128), F32),
            pltpu.SMEM((NONE,), jnp.int32),
            pltpu.SMEM((NONE,), jnp.int32),
            pltpu.SMEM((NONE,), jnp.int32),
            pltpu.SMEM((NONE,), jnp.int32),
            pltpu.SMEM((EXT + IN_BLK,), jnp.int32),
            dma((8,)),
            dma((2, NZ + 2)),
            dma((2, NY)),
            dma((2, NX)),
            dma((2, NX)),
            dma((2, 6)),
            dma((2, NX)),
            dma((2, NX)),
            dma((2, NY)),
            dma((2, NZ)),
        ],
        compiler_params=pltpu.CompilerParams(
            collective_id=0, has_side_effects=True, vmem_limit_bytes=60 * 1024 * 1024
        ),
    )(features, weight, rules, rule_counts, cotangent.reshape(1, OUT_BLK, br, co))


def solution(mesh):
    in_specs = (
        P("dp", "space", None),
        P(("dp", "space"), None),
        P("dp", "space", None, None),
        P("dp", "space"),
        P("dp", "space", None),
    )
    out_specs = (P("dp", "space", None), P("dp", "space", None), P(("dp", "space"), None))
    return jax.shard_map(local, mesh=mesh, in_specs=in_specs, out_specs=out_specs, check_vma=False)
```

time: 80.6 us -> 72.5 us (0.90)
  the two profiles are of different devices: /device:TPU:8 before, /device:TPU:1 now
where the time goes in v2:
time: 72.5 us; the launch traced here: 72 us
  Pallas kernels  68.2 us (94%)
  local copies, waits for them, and re-layouts  3.12 us (4%)
    pallas_call x1, Pallas kernels, local(): pl.pallas_call(kernel, out_shape=(jax.ShapeDtypeStruct(cotangent.shape, B...  68.2 us
    unnamed x7, local copies, waits for them, and re-layouts  3.12 us

profile of v2, /device:TPU:1, one launch (start us, length us, event | category | flops | bytes accessed | tf_op | source)
XLA Modules:
  0.0 72.0 jit_solution(5188295811850736112)
XLA Ops:
  0.6 68.2 %shard_map.76 = (bf16[1,512,256]{2,1,0:T(8,128)(2,1)}, bf16[1,1024,256]{2,1,0:T(8,128)(2,1)}, f32[4,256]{1,0:T(4,128)}) custom-call(bf16[1,1024,256]{2,1,0:T(8,128)(2,1)} %feat_hbm.1, bf16[4,256]{1,0:T(4,128)(2,1)} %w_hbm.1, s32[1,3,8,8]{3,2,1,0:T(8,128)} %bitcast.3, s32[1,8]{1,0:T(1,128)} %counts_hbm.1, bf16[1,4,128,256]{3,2,1,0:T(8,128)(2,1)} %bitcast.2), custom_call_target="tpu_custom_call" | custom-call | tf_op jit(solution)/shard_map/pallas_call | solution.py:355
  68.9 0.0 copy-start
  68.9 1.7 %copy.11 = bf16[1,512,256]{2,1,0:T(8,128)(2,1)} copy(bf16[1,512,256]{2,1,0:T(8,128)(2,1)} %get-tuple-element.6) | data formatting | bytes 524288
  70.6 0.0 copy-done
  70.6 0.0 copy-start.1
  70.6 0.8 %copy.12 = bf16[1,1024,256]{2,1,0:T(8,128)(2,1)} copy(bf16[1,1024,256]{2,1,0:T(8,128)(2,1)S(1)} %copy-done) | data formatting | bytes 1048576
  71.4 0.0 copy-done.1
  71.4 0.6 copy.13
Async XLA Ops:
  68.9 1.7 %copy-start = (bf16[1,1024,256]{2,1,0:T(8,128)(2,1)S(1)}, bf16[1,1024,256]{2,1,0:T(8,128)(2,1)}, u32[]{:S(2)}) copy-start(bf16[1,1024,256]{2,1,0:T(8,128)(2,1)} %get-tuple-element.7) | copy-start | bytes 1572868
  70.6 0.8 %copy-start.1 = (f32[4,256]{1,0:T(4,128)S(1)}, f32[4,256]{1,0:T(4,128)}, u32[]{:S(2)}) copy-start(f32[4,256]{1,0:T(4,128)} %get-tuple-element.8) | copy-start | bytes 12292

commit v3 on v2

--- a/solution.py
+++ b/solution.py
@@ -36,9 +36,9 @@
     feat_hbm, w_hbm, rules_hbm, counts_hbm, cot_hbm,
     act_hbm, gf_hbm, gw_hbm,
     xin, win, rules, counts, xp, xt, cot, wz, wst, wf, yb, sums, hs, hr, gext, act_ref, gf_ref, gw_ref,
-    sb_send, sb_recv, own, xs, xr, ys, yr, zs, zr,
+    sb_send, sb_recv, own, xs, xr, zs, zr,
     f_in, f_prev, b_slot, b_prev, lasts,
-    loc_sem, z_sem, y_sem, x_sem, c_sem, h_sem, rc_sem, rx_sem, ry_sem, rz_sem,
+    loc_sem, z_sem, xy_sem, c_sem, h_sem, rc_sem, rx_sem, rz_sem,
 ):
     ci = xin.shape[2]
     br = xp.shape[1]
@@ -55,11 +55,8 @@
     def x_of(off):
         return lax.rem(x + off, NX)
 
-    def at_x(off):
-        return (x_of(off) * 2 + c, space)
-
-    def at_y(off):
-        return (dp, z * NY + lax.rem(y + off, NY))
+    def at_xy(dx, dy):
+        return (x_of(dx) * 2 + c, z * NY + lax.rem(y + dy, NY))
 
     def at_z(off):
         return (dp, lax.rem(z + off, NZ) * NY + y)
@@ -70,6 +67,7 @@
             device_id=device, device_id_type=MESH,
         )
 
+    plane = [(dx, dy) for dx in (0, 1, 3, 2) for dy in range(NY) if dx or dy]
     pending = []
 
     def send(copy):
@@ -93,35 +91,29 @@
     def greet(device):
         pl.semaphore_signal(barrier, inc=1, device_id=device, device_id_type=MESH)
 
-    for d in (*range(1, REACH + 1), *range(NZ - REACH, NZ)):
+    for d in range(REACH, 0, -1):
         greet(at_z(d))
-    for d in range(1, NY):
-        greet(at_y(d))
-    for d in range(1, NX):
-        greet(at_x(d))
+        greet(at_z(NZ - d))
+    for dx, dy in plane:
+        greet(at_xy(dx, dy))
     for device in (sib, up, down):
         greet(device)
     get_w.wait()
     wz[0, 0:4, :] = win[:, 0:128].astype(F32)
     wz[0, 4:8, :] = win[:, 128:256].astype(F32)
-    pl.semaphore_wait(barrier, 2 * REACH + 1 + NY + NX)
+    pl.semaphore_wait(barrier, 2 * REACH + len(plane) + 3)
 
     def z_copy(d):
-        return remote(wz.at[0], wz.at[d], z_sem, d, at_z(d))
-
-    def each_z(act):
-        pl.loop(1, NZ)(act)
-
-    def z_pass(forward):
-        if forward:
-            src, dst, d = pl.ds(1, REACH), pl.ds(REACH + 1, REACH), REACH
-        else:
-            src, dst, d = pl.ds(NZ - REACH + 1, REACH - 1), pl.ds(NZ - 2 * REACH + 1, REACH - 1), NZ - REACH
-        return remote(wz.at[src], wz.at[dst], z_sem, NZ + int(forward), at_z(d))
-
-    for d in range(REACH, 0, -1):
+        slot = REACH - 1 + d if d > 0 else -d
+        return remote(wz.at[0], wz.at[slot], z_sem, slot, at_z(d % NZ))
+
+    def z_pass(above):
+        src, dst = pl.ds(0 if above else REACH, REACH), pl.ds((3 if above else 2) * REACH, REACH)
+        return remote(wz.at[src], wz.at[dst], z_sem, NZ + int(above), at_z(NZ - REACH if above else REACH))
+
+    near = [d for far in range(REACH, 0, -1) for d in (far, -far) if d > -REACH]
+    for d in near:
         send(z_copy(d))
-        send(z_copy(NZ - d))
 
     own_low, own_high = pl.ds(BND, BND), pl.ds(OUT_BLK, BND)
     top, bottom = pl.ds(BND + OUT_BLK, BND), pl.ds(0, BND)
@@ -135,7 +127,9 @@
 
     def channel(p):
         from_y = lax.rem(y + NY - lax.div(p, 4 * NZ), NY)
-        from_z = lax.rem(z + NZ - lax.div(lax.rem(p, 4 * NZ), 4), NZ)
+        tile = lax.div(lax.rem(p, 4 * NZ), 4)
+        up_by = jnp.where(tile < REACH, tile, jnp.where(tile < 3 * REACH, REACH - 1 - tile, tile - 2 * REACH))
+        from_z = lax.rem(z + NZ + up_by, NZ)
         return from_z * (4 * NY) + from_y * 4 + lax.rem(p, 4)
 
     perm = jnp.where(rows == channel(cols), 1.0, 0.0).astype(BF16)
@@ -149,6 +143,37 @@
 
     sums[NONE] = jnp.zeros(sums.shape[1:], F32)
     gext[EXT] = jnp.zeros(gext.shape[1:], BF16)
+
+    low = lax.broadcasted_iota(jnp.int32, (8, 128), 0) < 4
+    part = 4 * NZ
+
+    def unpack(half):
+        for p in range(half * NZ // 4, (half + 1) * NZ // 4):
+            a, b = wz[2 * p], wz[2 * p + 1]
+            wst[8 * p : 8 * p + 8, 0:128] = jnp.where(low, a, pltpu.roll(b, 4, 0))
+            wst[8 * p : 8 * p + 8, 128:256] = jnp.where(low, pltpu.roll(a, 4, 0), b)
+        rows = slice(half * part // 2, (half + 1) * part // 2)
+        wf[0, rows, :] = wst[rows, :].astype(BF16)
+
+    order = (0, 1, 3, 2)
+
+    def xy_copy(half, dx, dy):
+        start = half * part // 2
+        dst = wf.at[2 * order.index((NX - dx) % NX), pl.ds(dy * part + start, part // 2)]
+        index = (half * NX + dx) * NY + dy
+        return remote(wf.at[0, pl.ds(start, part // 2)], dst, xy_sem, index, at_xy(dx, dy))
+
+    def c_copy(off):
+        t = 2 * order.index(off)
+        return remote(wf.at[t], wf.at[t + 1], c_sem, off, sib)
+
+    for d in near:
+        z_copy(d).wait_recv()
+    send(z_pass(False))
+    send(z_pass(True))
+    unpack(0)
+    for dx, dy in plane:
+        send(xy_copy(0, dx, dy))
 
     def kernel_at(t):
         pair = t // 2
@@ -188,50 +213,20 @@
     for o in range(EXT + IN_BLK):
         lasts[o] = ends[o]
 
-    for d in range(1, REACH + 1):
-        z_copy(d).wait_recv()
-    send(z_pass(True))
-    for d in range(NZ - 1, NZ - REACH - 1, -1):
-        z_copy(d).wait_recv()
-    if REACH > 1:
-        send(z_pass(False))
-        z_pass(False).wait_recv()
+    z_pass(False).wait_recv()
     z_pass(True).wait_recv()
-
-    low = lax.broadcasted_iota(jnp.int32, (8, 128), 0) < 4
-    for p in range(NZ // 2):
-        a, b = wz[2 * p], wz[2 * p + 1]
-        wst[8 * p : 8 * p + 8, 0:128] = jnp.where(low, a, pltpu.roll(b, 4, 0))
-        wst[8 * p : 8 * p + 8, 128:256] = jnp.where(low, pltpu.roll(a, 4, 0), b)
-    part = 4 * NZ
-    wf[0, 0:part, :] = wst[...].astype(BF16)
-
-    def y_copy(d):
-        return remote(wf.at[0, pl.ds(0, part)], wf.at[0, pl.ds(d * part, part)], y_sem, d, at_y(d))
-
-    for d in range(1, NY):
-        send(y_copy(d))
-    for d in range(1, NY):
-        y_copy(d).wait_recv()
-
-    order = (0, 1, 3, 2)
-
-    def x_copy(d):
-        return remote(wf.at[0], wf.at[2 * order.index(NX - d)], x_sem, d, at_x(d))
-
-    def c_copy(off):
-        t = 2 * order.index(off)
-        return remote(wf.at[t], wf.at[t + 1], c_sem, off, sib)
-
-    for d in (1, 3, 2):
-        send(x_copy(d))
-    send(c_copy(0))
+    unpack(1)
+    for dx, dy in plane:
+        send(xy_copy(1, dx, dy))
 
     def arrive(off, other):
         if other:
             c_copy(off).wait_recv()
-        elif off:
-            x_copy(NX - off).wait_recv()
+        else:
+            for dy in range(NY):
+                if off or dy:
+                    xy_copy(0, (NX - off) % NX, dy).wait_recv()
+                    xy_copy(1, (NX - off) % NX, dy).wait_recv()
             send(c_copy(off))
 
     for t in range(OFFS):
@@ -242,31 +237,28 @@
             n = t * SLOTS + j
             sums[n] = yb[f_in[n]] + sums[f_prev[n]]
 
-    for i in range(EXT):
-        hs[i] = sums[lasts[i]].astype(BF16)
-
-    def rim_copy(half, upward):
-        src = (OUT_BLK if upward else 0) + BND * half
-        dst = src - OUT_BLK if upward else src + OUT_BLK
-        index = 2 + 2 * int(upward) + half
-        return remote(hs.at[pl.ds(src, BND)], hr.at[pl.ds(dst, BND)], h_sem, index, up if upward else down)
-
-    for half in (0, 1):
-        send(rim_copy(half, False))
-        send(rim_copy(half, True))
+    def rim_copy(i, upward):
+        src, dst = (i + OUT_BLK, i) if upward else (i, i + OUT_BLK)
+        index = 2 + OUT_BLK * int(upward) + i
+        return remote(hs.at[src], hr.at[dst], h_sem, index, up if upward else down)
+
+    for i in range(OUT_BLK):
+        for upward in (False, True):
+            o = i + OUT_BLK * int(upward)
+            hs[o] = sums[lasts[o]].astype(BF16)
+            send(rim_copy(i, upward))
     remote(cot.at[own_low], cot.at[top], h_sem, 0, down).wait_recv()
     remote(cot.at[own_high], cot.at[bottom], h_sem, 1, up).wait_recv()
-    for half in (0, 1):
-        for upward in (True, False):
-            rim_copy(half, upward).wait_recv()
-            first = (0 if upward else OUT_BLK) + BND * half
-            for o in range(first, first + BND):
-                pre = sums[lasts[o]] + hr[o].astype(F32)
-                sigma = jax.nn.sigmoid(pre)
-                if BND <= o < BND + OUT_BLK:
-                    act_ref[0, (o - BND) * br : (o - BND + 1) * br, :] = (pre * sigma).astype(BF16)
-                upstream = cot[o].astype(F32)
-                gext[o] = (upstream * sigma * (1.0 + pre * (1.0 - sigma))).astype(BF16)
+    for i in range(OUT_BLK):
+        for upward in (False, True):
+            rim_copy(i, upward).wait_recv()
+            o = i + (0 if upward else OUT_BLK)
+            pre = sums[lasts[o]] + hr[o].astype(F32)
+            sigma = jax.nn.sigmoid(pre)
+            if BND <= o < BND + OUT_BLK:
+                act_ref[0, (o - BND) * br : (o - BND + 1) * br, :] = (pre * sigma).astype(BF16)
+            upstream = cot[o].astype(F32)
+            gext[o] = (upstream * sigma * (1.0 + pre * (1.0 - sigma))).astype(BF16)
     put(act_ref, act_hbm, 5)
 
     def term(off, other):
@@ -278,6 +270,10 @@
     def to_sibling(off):
         sb_send[off] = term(off, True)
         send(remote(sb_send.at[off], sb_recv.at[off], rc_sem, off, sib))
+
+    def part_copy(dx, dy):
+        src = xs.at[dx, pl.ds((NY - dy) % NY * part, part)]
+        return remote(src, xr.at[dx * NY + dy], rx_sem, dx * NY + dy, at_xy(dx, dy))
 
     sequence = (2, 1, 3, 0)
     to_sibling(sequence[0])
@@ -286,11 +282,11 @@
         if i + 1 < NX:
             to_sibling(sequence[i + 1])
         remote(sb_send.at[off], sb_recv.at[off], rc_sem, off, sib).wait_recv()
-        if off:
-            xs[off] = (own[...] + sb_recv[off]).astype(BF16)
-            send(remote(xs.at[off], xr.at[off], rx_sem, off, at_x(off)))
-        else:
-            own[...] += sb_recv[off]
+        own[...] += sb_recv[off]
+        xs[off] = own[...].astype(BF16)
+        for dy in sorted(range(NY), key=lambda d: -min(d, NY - d)):
+            if off or dy:
+                send(part_copy(off, dy))
 
     for t in range(OFFS):
         flat = gext[0:EXT].reshape(EXT * br, gext.shape[2])
@@ -300,38 +296,34 @@
             place = jnp.minimum(b_slot[n], EXT - 1)
             sums[n] = yb[place] + sums[b_prev[n]]
 
-    for d in range(1, NX):
-        remote(xs.at[d], xr.at[d], rx_sem, d, at_x(d)).wait_recv()
-    total = own[...]
-    for d in range(1, NX):
-        total = total + xr[d].astype(F32)
-    own[...] = total
-    for d in range(1, NY):
-        ys[d] = own[(NY - d) * part : (NY - d + 1) * part, :].astype(BF16)
-        send(remote(ys.at[d], yr.at[d], ry_sem, d, at_y(d)))
-
     for i in range(IN_BLK):
         back = sums[lasts[EXT + i]][:, 0:ci].astype(BF16)
         gf_ref[0, i * br : (i + 1) * br, :] = dot(back, perm_t, NN).astype(BF16)
 
     put(gf_ref, gf_hbm, 6)
 
-    for d in range(1, NY):
-        remote(ys.at[d], yr.at[d], ry_sem, d, at_y(d)).wait_recv()
     total = own[0:part, :]
-    for d in range(1, NY):
-        total = total + yr[d].astype(F32)
+    for dx, dy in plane:
+        part_copy(dx, dy).wait_recv()
+    for dx, dy in plane:
+        total = total + xr[dx * NY + dy].astype(F32)
     for p in range(NZ // 2):
         a, b = total[8 * p : 8 * p + 8, 0:128], total[8 * p : 8 * p + 8, 128:256]
         zs[2 * p] = jnp.where(low, a, pltpu.roll(b, 4, 0))
         zs[2 * p + 1] = jnp.where(low, pltpu.roll(a, 4, 0), b)
 
     def out_copy(d):
-        return remote(zs.at[NZ - d], zr.at[d], rz_sem, d, at_z(d))
-
-    each_z(lambda d: out_copy(d).start())
-    pending.append(lambda: each_z(lambda d: out_copy(d).wait_send()))
-    each_z(lambda d: out_copy(d).wait_recv())
+        if d < 2 * REACH:
+            tile = d if d < REACH else d + 2 * REACH
+        else:
+            tile = REACH - 1 + NZ - d
+        return remote(zs.at[tile], zr.at[d], rz_sem, d, at_z(d))
+
+    far_first = sorted(range(1, NZ), key=lambda d: -min(d, NZ - d))
+    for d in far_first:
+        send(out_copy(d))
+    for d in range(1, NZ):
+        out_copy(d).wait_recv()
 
     total = zs[0]
     for d in range(1, NZ):
@@ -384,9 +376,7 @@
             V((NX, ci, co), F32),
             V((ci, co), F32),
             V((NX, ci, co), BF16),
-            V((NX, ci, co), BF16),
-            V((NY, 4 * NZ, co), BF16),
-            V((NY, 4 * NZ, co), BF16),
+            V((NX * NY, 4 * NZ, co), BF16),
             V((NZ, 8, 128), F32),
             V((NZ, 8, 128), F32),
             pltpu.SMEM((NONE,), jnp.int32),
@@ -396,13 +386,11 @@
             pltpu.SMEM((EXT + IN_BLK,), jnp.int32),
             dma((8,)),
             dma((2, NZ + 2)),
-            dma((2, NY)),
+            dma((2, 2 * NX * NY)),
             dma((2, NX)),
+            dma((2, 2 + 2 * OUT_BLK)),
             dma((2, NX)),
-            dma((2, 6)),
-            dma((2, NX)),
-            dma((2, NX)),
-            dma((2, NY)),
+            dma((2, NX * NY)),
             dma((2, NZ)),
         ],
         compiler_params=pltpu.CompilerParams(

time: 72.5 us -> 66.5 us (0.917)
  Pallas kernels: 68.2 us -> 62.6 us
    pallas_call x1, Pallas kernels: 68.2 us -> 62.6 us  [local(): pl.pallas_call(kernel, out_shape=(jax.ShapeDtypeStruct(cotangent.shape, B...]
where the time goes in v3:
time: 66.5 us; the launch traced here: 66.4 us
  Pallas kernels  62.6 us (94%)
  local copies, waits for them, and re-layouts  3.12 us (5%)
    pallas_call x1, Pallas kernels, local(): pl.pallas_call(kernel, out_shape=(jax.ShapeDtypeStruct(cotangent.shape, B...  62.6 us
    unnamed x7, local copies, waits for them, and re-layouts  3.12 us

profile of v3, /device:TPU:1, one launch (start us, length us, event | category | flops | bytes accessed | tf_op | source)
XLA Modules:
  0.0 66.4 jit_solution(5802310384414201097)
XLA Ops:
  0.6 62.6 %shard_map.76 = (bf16[1,512,256]{2,1,0:T(8,128)(2,1)}, bf16[1,1024,256]{2,1,0:T(8,128)(2,1)}, f32[4,256]{1,0:T(4,128)}) custom-call(bf16[1,1024,256]{2,1,0:T(8,128)(2,1)} %feat_hbm.1, bf16[4,256]{1,0:T(4,128)(2,1)} %w_hbm.1, s32[1,3,8,8]{3,2,1,0:T(8,128)} %bitcast.3, s32[1,8]{1,0:T(1,128)} %counts_hbm.1, bf16[1,4,128,256]{3,2,1,0:T(8,128)(2,1)} %bitcast.2), custom_call_target="tpu_custom_call" | custom-call | tf_op jit(solution)/shard_map/pallas_call | solution.py:347
  63.2 0.0 copy-start
  63.3 1.7 %copy.11 = bf16[1,512,256]{2,1,0:T(8,128)(2,1)} copy(bf16[1,512,256]{2,1,0:T(8,128)(2,1)} %get-tuple-element.6) | data formatting | bytes 524288
  65.0 0.0 copy-done
  65.0 0.0 copy-start.1
  65.0 0.8 %copy.12 = bf16[1,1024,256]{2,1,0:T(8,128)(2,1)} copy(bf16[1,1024,256]{2,1,0:T(8,128)(2,1)S(1)} %copy-done) | data formatting | bytes 1048576
  65.8 0.0 copy-done.1
  65.8 0.6 copy.13
Async XLA Ops:
  63.2 1.7 %copy-start = (bf16[1,1024,256]{2,1,0:T(8,128)(2,1)S(1)}, bf16[1,1024,256]{2,1,0:T(8,128)(2,1)}, u32[]{:S(2)}) copy-start(bf16[1,1024,256]{2,1,0:T(8,128)(2,1)} %get-tuple-element.7) | copy-start | bytes 1572868
  65.0 0.8 %copy-start.1 = (f32[4,256]{1,0:T(4,128)S(1)}, f32[4,256]{1,0:T(4,128)}, u32[]{:S(2)}) copy-start(f32[4,256]{1,0:T(4,128)} %get-tuple-element.8) | copy-start | bytes 12292

commit v4 on v3

--- a/solution.py
+++ b/solution.py
@@ -1,5 +1,3 @@
-import functools
-
 import jax
 import jax.numpy as jnp
 from jax import lax
@@ -35,13 +33,13 @@
 def kernel(
     feat_hbm, w_hbm, rules_hbm, counts_hbm, cot_hbm,
     act_hbm, gf_hbm, gw_hbm,
-    xin, win, rules, counts, xp, xt, cot, wz, wst, wf, yb, sums, hs, hr, gext, act_ref, gf_ref, gw_ref,
+    xin, win, rules, counts, xp, xt, cot, wz, wst, wf, sums, hs, hr, gext, act_ref, gf_ref, gw_ref,
     sb_send, sb_recv, own, xs, xr, zs, zr,
     f_in, f_prev, b_slot, b_prev, lasts,
     loc_sem, z_sem, xy_sem, c_sem, h_sem, rc_sem, rx_sem, rz_sem,
 ):
     ci = xin.shape[2]
-    br = xp.shape[1]
+    br, co = xp.shape[1], wf.shape[2]
     dp = lax.axis_index("dp")
     space = lax.axis_index("space")
     x, c = lax.div(dp, 2), lax.rem(dp, 2)
@@ -67,7 +65,7 @@
             device_id=device, device_id_type=MESH,
         )
 
-    plane = [(dx, dy) for dx in (0, 1, 3, 2) for dy in range(NY) if dx or dy]
+    plane = [(dx, dy) for dx in (0, 1, 3, 2) for dy in (2, 1, 3, 0) if dx or dy]
     pending = []
 
     def send(copy):
@@ -114,12 +112,6 @@
     near = [d for far in range(REACH, 0, -1) for d in (far, -far) if d > -REACH]
     for d in near:
         send(z_copy(d))
-
-    own_low, own_high = pl.ds(BND, BND), pl.ds(OUT_BLK, BND)
-    top, bottom = pl.ds(BND + OUT_BLK, BND), pl.ds(0, BND)
-    get_cot.wait()
-    send(remote(cot.at[own_low], cot.at[top], h_sem, 0, down))
-    send(remote(cot.at[own_high], cot.at[bottom], h_sem, 1, up))
 
     get_x.wait()
     rows = lax.broadcasted_iota(jnp.int32, (ci, ci), 0)
@@ -229,13 +221,19 @@
                     xy_copy(1, (NX - off) % NX, dy).wait_recv()
             send(c_copy(off))
 
+    own_low, own_high = pl.ds(BND, BND), pl.ds(OUT_BLK, BND)
+    top, bottom = pl.ds(BND + OUT_BLK, BND), pl.ds(0, BND)
     for t in range(OFFS):
+        if t == OFFS // 2:
+            get_cot.wait()
+            send(remote(cot.at[own_low], cot.at[top], h_sem, 0, down))
+            send(remote(cot.at[own_high], cot.at[bottom], h_sem, 1, up))
         arrive(order[t // 2], t % 2 == 1)
-        flat = xp[...].reshape(IN_BLK * br, ci)
-        yb[...] = dot(flat, wf[t], NN).reshape(yb.shape)
+        picked = [xp[f_in[t * SLOTS + j]] for j in range(SLOTS)]
+        products = dot(jnp.concatenate(picked, axis=0), wf[t], NN)
         for j in range(SLOTS):
             n = t * SLOTS + j
-            sums[n] = yb[f_in[n]] + sums[f_prev[n]]
+            sums[n, :, 0:co] = products[j * br : (j + 1) * br] + sums[f_prev[n]][:, 0:co]
 
     def rim_copy(i, upward):
         src, dst = (i + OUT_BLK, i) if upward else (i, i + OUT_BLK)
@@ -288,19 +286,15 @@
             if off or dy:
                 send(part_copy(off, dy))
 
-    for t in range(OFFS):
-        flat = gext[0:EXT].reshape(EXT * br, gext.shape[2])
-        yb[:, :, 0:ci] = dot(flat, wf[t], NT).reshape(EXT, br, ci)
+    def back(t):
+        picked = [gext[b_slot[t * SLOTS + j]] for j in range(SLOTS)]
+        products = dot(jnp.concatenate(picked, axis=0), wf[t], NT)
         for j in range(SLOTS):
             n = t * SLOTS + j
-            place = jnp.minimum(b_slot[n], EXT - 1)
-            sums[n] = yb[place] + sums[b_prev[n]]
-
-    for i in range(IN_BLK):
-        back = sums[lasts[EXT + i]][:, 0:ci].astype(BF16)
-        gf_ref[0, i * br : (i + 1) * br, :] = dot(back, perm_t, NN).astype(BF16)
-
-    put(gf_ref, gf_hbm, 6)
+            sums[n, :, 0:ci] = products[j * br : (j + 1) * br] + sums[b_prev[n]][:, 0:ci]
+
+    for t in range(OFFS // 2):
+        back(t)
 
     total = own[0:part, :]
     for dx, dy in plane:
@@ -322,6 +316,17 @@
     far_first = sorted(range(1, NZ), key=lambda d: -min(d, NZ - d))
     for d in far_first:
         send(out_copy(d))
+
+    for t in range(OFFS // 2, OFFS):
+        back(t)
+    for i in range(IN_BLK):
+        ready = sums[lasts[EXT + i]][:, 0:ci].astype(BF16)
+        gf_ref[0, i * br : (i + 1) * br, :] = dot(ready, perm_t, NN).astype(BF16)
+    put(gf_ref, gf_hbm, 6)
+    for wait in pending:
+        wait()
+    pending.clear()
+
     for d in range(1, NZ):
         out_copy(d).wait_recv()
 
@@ -335,6 +340,19 @@
     put(gw_ref, gw_hbm, 7)
     for wait in pending:
         wait()
+
+
+def hand_over(act, gf, gw, act_out, gf_out, gw_out, act_here, gf_here, gw_here, sems):
+    arrays = ((act, act_here, act_out), (gf, gf_here, gf_out), (gw, gw_here, gw_out))
+    into = [pltpu.make_async_copy(a, here, sems.at[0, i]) for i, (a, here, _) in enumerate(arrays)]
+    out = [pltpu.make_async_copy(here, b, sems.at[1, i]) for i, (_, here, b) in enumerate(arrays)]
+    for copy in into:
+        copy.start()
+    for first, then in zip(into, out):
+        first.wait()
+        then.start()
+    for copy in out:
+        copy.wait()
 
 
 def local(features, weight, rulebook, rule_counts, cotangent):
@@ -344,7 +362,7 @@
     rules = jnp.transpose(rulebook, (0, 2, 1, 3))
     dma = pltpu.SemaphoreType.DMA
     V = pltpu.VMEM
-    return pl.pallas_call(
+    results = pl.pallas_call(
         kernel,
         out_shape=(
             jax.ShapeDtypeStruct(cotangent.shape, BF16),
@@ -364,7 +382,6 @@
             V((NZ, 8, 128), F32),
             V((4 * NZ, co), F32),
             V((OFFS, ci, co), BF16),
-            V((IN_BLK, br, max(ci, co)), F32),
             V((NONE + 1, br, max(ci, co)), F32),
             V((EXT, br, co), BF16),
             V((EXT, br, co), BF16),
@@ -397,6 +414,14 @@
             collective_id=0, has_side_effects=True, vmem_limit_bytes=60 * 1024 * 1024
         ),
     )(features, weight, rules, rule_counts, cotangent.reshape(1, OUT_BLK, br, co))
+    return pl.pallas_call(
+        hand_over,
+        out_shape=tuple(jax.ShapeDtypeStruct(r.shape, r.dtype) for r in results),
+        in_specs=[hbm] * 3,
+        out_specs=(hbm,) * 3,
+        scratch_shapes=[V(r.shape, r.dtype) for r in results] + [dma((2, 3))],
+        compiler_params=pltpu.CompilerParams(vmem_limit_bytes=60 * 1024 * 1024),
+    )(*results)
 
 
 def solution(mesh):

time: 66.5 us -> 64.7 us (0.973)
  local copies, waits for them, and re-layouts: 3.12 us -> 0 us
  Pallas kernels: 62.6 us -> 63.9 us
    unnamed x7 -> x0, local copies, waits for them, and re-layouts: 3.12 us -> none
    pallas_call x0 -> x1, Pallas kernels: none -> 1.97 us  [local(): pl.pallas_call(hand_over, out_shape=tuple((jax.ShapeDtypeStruct(r.shape,...]
where the time goes in v4:
time: 64.7 us; the launch traced here: 64.6 us
  Pallas kernels  63.9 us (99%)
    pallas_call x1, Pallas kernels, local(): pl.pallas_call(kernel, out_shape=(jax.ShapeDtypeStruct(cotangent.shape, B...  62 us
    pallas_call x1, Pallas kernels, local(): pl.pallas_call(hand_over, out_shape=tuple((jax.ShapeDtypeStruct(r.shape,...  1.97 us

profile of v4, /device:TPU:1, one launch (start us, length us, event | category | flops | bytes accessed | tf_op | source)
XLA Modules:
  0.0 64.6 jit_solution(5129275088419693734)
XLA Ops:
  0.6 62.0 %shard_map.76 = (bf16[1,512,256]{2,1,0:T(8,128)(2,1)}, bf16[1,1024,256]{2,1,0:T(8,128)(2,1)}, f32[4,256]{1,0:T(4,128)}) custom-call(bf16[1,1024,256]{2,1,0:T(8,128)(2,1)} %feat_hbm.1, bf16[4,256]{1,0:T(4,128)(2,1)} %w_hbm.1, s32[1,3,8,8]{3,2,1,0:T(8,128)} %bitcast.3, s32[1,8]{1,0:T(1,128)} %counts_hbm.1, bf16[1,4,128,256]{3,2,1,0:T(8,128)(2,1)} %bitcast.2), custom_call_target="tpu_custom_call" | custom-call | tf_op jit(solution)/shard_map/pallas_call | solution.py:365
  62.6 2.0 %shard_map.77 = (bf16[1,512,256]{2,1,0:T(8,128)(2,1)}, bf16[1,1024,256]{2,1,0:T(8,128)(2,1)}, f32[4,256]{1,0:T(4,128)}) custom-call(bf16[1,512,256]{2,1,0:T(8,128)(2,1)} %get-tuple-element.6.act, bf16[1,1024,256]{2,1,0:T(8,128)(2,1)} %get-tuple-element.7.gf, f32[4,256]{1,0:T(4,128)} %get-tuple-element.8.gw), custom_call_target="tpu_custom_call" | custom-call | tf_op jit(solution)/shard_map/pallas_call | solution.py:417

commit v5 on v4

--- a/solution.py
+++ b/solution.py
@@ -224,9 +224,10 @@
     own_low, own_high = pl.ds(BND, BND), pl.ds(OUT_BLK, BND)
     top, bottom = pl.ds(BND + OUT_BLK, BND), pl.ds(0, BND)
     for t in range(OFFS):
-        if t == OFFS // 2:
+        if t == OFFS // 2 - 1:
             get_cot.wait()
             send(remote(cot.at[own_low], cot.at[top], h_sem, 0, down))
+        if t == OFFS // 2:
             send(remote(cot.at[own_high], cot.at[bottom], h_sem, 1, up))
         arrive(order[t // 2], t % 2 == 1)
         picked = [xp[f_in[t * SLOTS + j]] for j in range(SLOTS)]
@@ -252,7 +253,7 @@
             rim_copy(i, upward).wait_recv()
             o = i + (0 if upward else OUT_BLK)
             pre = sums[lasts[o]] + hr[o].astype(F32)
-            sigma = jax.nn.sigmoid(pre)
+            sigma = 0.5 + 0.5 * jnp.tanh(0.5 * pre)
             if BND <= o < BND + OUT_BLK:
                 act_ref[0, (o - BND) * br : (o - BND + 1) * br, :] = (pre * sigma).astype(BF16)
             upstream = cot[o].astype(F32)

time: 64.7 us -> 64.7 us (level)
  no operation moved by 1% of the time
where the time goes in v5:
time: 64.7 us; the launch traced here: 64.6 us
  Pallas kernels  63.9 us (99%)
    pallas_call x1, Pallas kernels, local(): pl.pallas_call(kernel, out_shape=(jax.ShapeDtypeStruct(cotangent.shape, B...  62 us
    pallas_call x1, Pallas kernels, local(): pl.pallas_call(hand_over, out_shape=tuple((jax.ShapeDtypeStruct(r.shape,...  1.97 us

profile of v5, /device:TPU:1, one launch (start us, length us, event | category | flops | bytes accessed | tf_op | source)
XLA Modules:
  0.0 64.6 jit_solution(2873174962848332333)
XLA Ops:
  0.6 62.0 %shard_map.76 = (bf16[1,512,256]{2,1,0:T(8,128)(2,1)}, bf16[1,1024,256]{2,1,0:T(8,128)(2,1)}, f32[4,256]{1,0:T(4,128)}) custom-call(bf16[1,1024,256]{2,1,0:T(8,128)(2,1)} %feat_hbm.1, bf16[4,256]{1,0:T(4,128)(2,1)} %w_hbm.1, s32[1,3,8,8]{3,2,1,0:T(8,128)} %bitcast.3, s32[1,8]{1,0:T(1,128)} %counts_hbm.1, bf16[1,4,128,256]{3,2,1,0:T(8,128)(2,1)} %bitcast.2), custom_call_target="tpu_custom_call" | custom-call | tf_op jit(solution)/shard_map/pallas_call | solution.py:366
  62.6 2.0 %shard_map.77 = (bf16[1,512,256]{2,1,0:T(8,128)(2,1)}, bf16[1,1024,256]{2,1,0:T(8,128)(2,1)}, f32[4,256]{1,0:T(4,128)}) custom-call(bf16[1,512,256]{2,1,0:T(8,128)(2,1)} %get-tuple-element.6.act, bf16[1,1024,256]{2,1,0:T(8,128)(2,1)} %get-tuple-element.7.gf, f32[4,256]{1,0:T(4,128)} %get-tuple-element.8.gw), custom_call_target="tpu_custom_call" | custom-call | tf_op jit(solution)/shard_map/pallas_call | solution.py:418
